TPU v7x, 32 devices: a whole 2x2x4 slice. The times are simulated.
32 devices in a mesh: gx: 8 (over z, y), gy: 4 (over x, core).
Axes of the slice: x: 2, y: 2, z: 4, core: 2. Of those that a mesh axis runs over, the one named last changes fastest.
Arguments:
- jitter: float32 [4096, 3, 128], P(('gx', 'gy')), may hold values from -0.2 to 0.2
- displacement: float32 [4096, 3, 128], P(('gx', 'gy')), may hold values from -0.1 to 0.1
- modulus: float32 [4096, 128], P(('gx', 'gy')), may hold values from 0.1 to 1
- start_vec: float32 [4096, 3, 128], P(('gx', 'gy')), may hold values from -6 to 6
- old_home: int32 [4096], P(('gx', 'gy')), may hold values from 0 to 4095, as said below
- ghost_send: int32 [32, 9, 16], P(('gx', 'gy')), may hold values from -1 to 127, as said below
- pair_list: int32 [32, 4, 512], P(('gx', 'gy')), may hold values from -1 to 271, as said below
- pair_count: int32 [32], P(('gx', 'gy')), may hold values from 64 to 512, as said below
- broken: int32 [16384, 16, 128], P(('gx', 'gy')), may hold values from 0 to 255
Outputs:
- first_image: float32 [4096, 3, 128], P(('gx', 'gy'))
- second_image: float32 [4096, 3, 128], P(('gx', 'gy'))
Inputs may be any that keep to these rules, and one draw needn't show every extreme that they name: `old_home`: A permutation. Row i of the old layout and row j of the rebalanced layout belong to devices i // 128 and j // 128; each device hands exactly 16 of its old tiles to each device beside it along gx or along gy (grid places differing by one in one coordinate, no wrap) and keeps the others. `ghost_send`: directions whose receiver lies outside the grid, and direction 4, hold only -1; for every other direction the first 1 to 16 slots hold rows below 128 and the rest -1; every device fills all 16 slots toward some neighbour along gx or gy. `pair_list`: tile is below 128; partner is below 128, or 128 + e * 16 + k where the device at offset (e // 3 - 1, e mod 3 - 1) exists and its slot k toward this device holds a row; shifts are -1, 0 or 1; when both shifts are 0, partner equals tile. Slots past the count are filled the same way. `pair_count`: at least 64; some device has 512.
All inputs are finite; a program needn't handle non-finite values.
Results may differ from a plain program's by a relative error of at most 0.0003.
Values sent between devices are 32-bit elements; how exact they have to be, the bound alone decides.
A program may use at most 64 MiB of HBM per device.

v0:
```python
import functools
import jax
import jax.numpy as jnp
from jax import lax
from jax.experimental import pallas as pl
from jax.experimental.pallas import tpu as pltpu
from jax.sharding import PartitionSpec as P

CAP = 16
F32 = jnp.float32
VMEM = pl.BlockSpec(memory_space=pltpu.VMEM)
SMEM = pl.BlockSpec(memory_space=pltpu.SMEM)
LIMIT = pltpu.CompilerParams(vmem_limit_bytes=48 * 1024 * 1024)
DIRS = (0, 1, 2, 3, 5, 6, 7, 8)
FIELDS = (0, 1, 2, 3, 4, 5, 6, 8, 9, 10)


def lattice(points):
    counter = jnp.arange(points, dtype=jnp.int32)
    return jnp.stack([counter % 8, counter // 8 % (points // 16), counter // (points // 2)]).astype(F32)


def hand_kernel(asked, jit, disp, mod, vec, *outs):
    for out in outs:
        out[...] = jnp.zeros_like(out)

    def body(i, carry):
        for d, out in enumerate(outs):
            row = asked[d, i]
            out[i, 0:3] = jit[row]
            out[i, 3:6] = disp[row]
            out[i, 6:7] = mod[pl.ds(row, 1)]
            out[i, 8:11] = vec[row]
        return carry

    lax.fori_loop(0, CAP, body, 0)


def settle_kernel(pick, send, lat8, jit, disp, mod, vec, in0, in1, in2, in3, local, *rest):
    outs, pool = rest[:8], rest[8]
    rows = jit.shape[0]
    pool[0:rows] = jnp.zeros((rows,) + pool.shape[1:], F32)
    pool[0:rows, 0:3, :] = jit[...]
    pool[0:rows, 3:6, :] = disp[...]
    pool[0:rows, 8:11, :] = vec[...]

    def put_mod(j, carry):
        pool[j, 6:7, :] = mod[pl.ds(j, 1)]
        return carry

    lax.fori_loop(0, rows, put_mod, 0, unroll=8)
    for d, arrived in enumerate((in0, in1, in2, in3)):
        pool[rows + d * CAP : rows + (d + 1) * CAP] = arrived[...]
    points = jit.shape[2]
    sub = lax.broadcasted_iota(jnp.int32, (8, points), 0)
    scale = jnp.where(sub == 6, 0.05, 1.0)
    moved = (sub >= 3) & (sub < 6)

    def settle(j, carry):
        held = pool[pick[j]]
        low = held[0:8]
        base = low + lat8[...]
        shifted = jnp.where(moved, pltpu.roll(base, 3, 0), 0.0)
        local[j, 0:8] = low * scale + jnp.where(moved, 0.0, lat8[...]) + shifted
        local[j, 8:16] = held[8:16]
        return carry

    lax.fori_loop(0, rows, settle, 0, unroll=8)

    def ghosts(i, carry):
        for c, out in zip(DIRS, outs):
            out[i] = local[jnp.maximum(send[c, i], 0)]
        return carry

    lax.fori_loop(0, outs[0].shape[0], ghosts, 0)


def apply_kernel(first, pairs, order, bounds, send, spread, words, local, *rest):
    ghosts, rest = rest[:8], rest[8:]
    if not first:
        field, field_ghosts, rest = rest[0], rest[1:9], rest[9:]
    image, rest = rest[0], rest[1:]
    if first:
        sends, rest = rest[:8], rest[8:]
    full, turned, total = rest
    rows, _, points = local.shape
    cap = ghosts[0].shape[0]
    full[0:rows] = local[...]
    full[rows + 4 * cap : rows + 5 * cap] = jnp.zeros((cap,) + full.shape[1:], F32)
    for e, ghost in zip(DIRS, ghosts):
        full[rows + e * cap : rows + (e + 1) * cap] = ghost[...]
    if not first:
        full[0:rows, 8:11, :] = field[...]
        for e, ghost in zip(DIRS, field_ghosts):
            full[rows + e * cap : rows + (e + 1) * cap, 8:16, :] = ghost[...]

    def turn(j, carry):
        state = full[j]
        high = state.astype(jnp.bfloat16).astype(F32)
        rest_of = state - high
        middle = rest_of.astype(jnp.bfloat16).astype(F32)
        turned[j] = jnp.transpose(jnp.concatenate([high, middle, rest_of - middle], axis=0))
        return carry

    lax.fori_loop(0, full.shape[0], turn, 0, unroll=8)
    total[...] = jnp.zeros_like(total)

    def bonds(side_b, side_a, flags, acc, guard):
        part = lambda c: side_b[FIELDS.index(c)]
        xi = [part(c) - side_a[c] for c in range(3)]
        y = [part(3 + c) - side_a[3 + c] for c in range(3)]
        dv = [part(8 + c) - side_a[8 + c] for c in range(3)]
        r2 = xi[0] * xi[0] + xi[1] * xi[1] + xi[2] * xi[2]
        l2 = y[0] * y[0] + y[1] * y[1] + y[2] * y[2]
        weight = jnp.maximum(1.0 - r2 * (1.0 / 9.0), 0.0)
        c = (part(6) + side_a[6]) * jnp.where(flags == 0, weight, 0.0)
        if guard:
            c = jnp.where(r2 < 1e-2, 0.0, c)
            r2 = jnp.maximum(r2, 1e-2)
            l2 = jnp.maximum(l2, 1e-2)
        r_inv = lax.rsqrt(r2)
        l_inv = lax.rsqrt(l2)
        cl = c * l_inv
        k2 = c * r_inv - cl
        along = cl * (l_inv * l_inv) * (y[0] * dv[0] + y[1] * dv[1] + y[2] * dv[2])
        return [acc[i] + (k2 * dv[i] + along * y[i]) for i in range(3)]

    def pair(kind, slot):
        live = slot >= 0
        q = jnp.maximum(slot, 0)
        tile = pairs[0, q]
        partner = pairs[1, q]
        sx = pairs[2, q]
        sy = pairs[3, q]
        dx = (sx * 8).astype(F32)
        dy = (sy * (points // 16)).astype(F32)
        side_a = []
        for c in range(11):
            if c == 7:
                side_a.append(None)
                continue
            row = full[tile, c : c + 1]
            if c in (0, 3) and kind & 1:
                row = row - dx
            if c in (1, 4) and kind & 2:
                row = row - dy
            side_a.append(jnp.broadcast_to(row, (8, points)))
        blocks, words_of = [], []
        x0 = jnp.where(sx > 0, 0, 5) if kind & 1 else 0
        if kind < 2:
            for k in range(3 if kind else 8):
                for z in range(2):
                    block = turned[partner, pl.ds(x0 + k + 64 * z, 8, stride=8), :]
                    flags = words[q, 8 * z : 8 * z + 8] & jnp.left_shift(1, x0 + k)
                    blocks.append(block)
                    words_of.append(flags)
        elif kind == 2:
            y0 = jnp.where(sy > 0, 0, 5)
            bit = jnp.left_shift(1, lax.broadcasted_iota(jnp.int32, (8, points), 0))
            for k in range(3):
                for z in range(2):
                    start = (y0 + k) * 8 + 64 * z
                    block = turned[partner, pl.ds(pl.multiple_of(start, 8), 8), :]
                    word = jnp.broadcast_to(words[q, pl.ds(y0 + k + 8 * z, 1), :], (8, points))
                    blocks.append(block)
                    words_of.append(word & bit)
        else:
            y0 = jnp.where(sy > 0, 0, 4)
            word = jnp.concatenate([words[q, pl.ds(y0, 4), :], words[q, pl.ds(y0 + 8, 4), :]], axis=0)
            for k in range(3):
                start = x0 + k + 8 * y0
                block = jnp.concatenate(
                    [
                        turned[partner, pl.ds(start, 4, stride=8), :],
                        turned[partner, pl.ds(start + 64, 4, stride=8), :],
                    ],
                    axis=0,
                )
                blocks.append(block)
                words_of.append(word & jnp.left_shift(1, x0 + k))
        return live, tile, side_a, blocks, words_of

    for kind, width in enumerate(UNROLL):

        def step(i, carry, kind=kind, width=width):
            batch = [pair(kind, order[i * width + u]) for u in range(width)]
            stacked = jnp.concatenate([b for one in batch for b in one[3]], axis=0)
            wide = jnp.dot(stacked.astype(jnp.bfloat16), spread[...], preferred_element_type=F32)
            at = 0
            done = []
            for live, tile, side_a, blocks, words_of in batch:
                acc = [jnp.zeros((8, points), F32)] * 3
                for flags in words_of:
                    side_b = [wide[at : at + 8, n * points : (n + 1) * points] for n in range(len(FIELDS))]
                    acc = bonds(side_b, side_a, flags, acc, kind == 0)
                    at += 8
                done.append((tile, [jnp.where(live, term, 0.0) for term in acc]))
            for tile, acc in done:
                for c in range(3):
                    total[tile, c] += acc[c]
            return carry

        lax.fori_loop(bounds[2 * kind], bounds[2 * kind + 1], step, 0)

    def close(j, carry):
        image[j] = jnp.sum(total[j], axis=1)
        return carry

    lax.fori_loop(0, rows, close, 0, unroll=4)
    if first:
        for out in sends:
            out[...] = jnp.zeros_like(out)

        def ghost_rows(i, carry):
            for c, out in zip(DIRS, sends):
                out[i, 0:3] = image[jnp.maximum(send[c, i], 0)]
            return carry

        lax.fori_loop(0, cap, ghost_rows, 0)


def exchange_kernel(offsets, *refs):
    n = len(offsets)
    ins, outs, send_sem, recv_sem = refs[:n], refs[n : 2 * n], refs[2 * n], refs[2 * n + 1]
    n_x, n_y = lax.axis_size("gx"), lax.axis_size("gy")
    x, y = lax.axis_index("gx"), lax.axis_index("gy")

    def exists(ox, oy):
        return (x + ox >= 0) & (x + ox < n_x) & (y + oy >= 0) & (y + oy < n_y)

    barrier = pltpu.get_barrier_semaphore()
    for ox, oy in offsets:

        @pl.when(exists(ox, oy))
        def _():
            pl.semaphore_signal(
                barrier, inc=1, device_id=(x + ox, y + oy), device_id_type=pl.DeviceIdType.MESH
            )

    peers = sum(jnp.where(exists(ox, oy), 1, 0) for ox, oy in offsets)
    pl.semaphore_wait(barrier, peers)

    def copy(d):
        ox, oy = offsets[d]
        back = offsets.index((-ox, -oy))
        return pltpu.make_async_remote_copy(
            src_ref=ins[d],
            dst_ref=outs[back],
            send_sem=send_sem.at[d],
            recv_sem=recv_sem.at[back],
            device_id=(x + ox, y + oy),
            device_id_type=pl.DeviceIdType.MESH,
        )

    for d, (ox, oy) in enumerate(offsets):

        @pl.when(exists(ox, oy))
        def _():
            copy(d).start()

        @pl.when(jnp.logical_not(exists(ox, oy)))
        def _():
            outs[d][...] = jnp.zeros_like(outs[d])

    for d, (ox, oy) in enumerate(offsets):

        @pl.when(exists(ox, oy))
        def _():
            copy(d).wait_send()
            copy(offsets.index((-ox, -oy))).wait_recv()


def exchange(blocks, offsets, ident):
    n = len(offsets)
    return pl.pallas_call(
        functools.partial(exchange_kernel, offsets),
        out_shape=[jax.ShapeDtypeStruct(b.shape, b.dtype) for b in blocks],
        in_specs=[VMEM] * n,
        out_specs=[VMEM] * n,
        scratch_shapes=[pltpu.SemaphoreType.DMA((n,)), pltpu.SemaphoreType.DMA((n,))],
        compiler_params=pltpu.CompilerParams(
            collective_id=ident, has_side_effects=True, vmem_limit_bytes=16 * 1024 * 1024
        ),
    )(*blocks)


SIDES = ((-1, 0), (1, 0), (0, -1), (0, 1))
AROUND = tuple((e // 3 - 1, e % 3 - 1) for e in DIRS)
UNROLL = (1, 4, 4, 8)


def by_kind(pair_list, count):
    pairs = pair_list.shape[1]
    slot = jnp.arange(pairs, dtype=jnp.int32)
    kind = (pair_list[2] != 0).astype(jnp.int32) + 2 * (pair_list[3] != 0).astype(jnp.int32)
    kind = jnp.where(slot < count, kind, 4)
    earlier = (kind[:, None] == kind[None, :]) & (slot[:, None] < slot[None, :])
    place = jnp.sum(earlier.astype(jnp.int32), axis=0)
    start, bounds = jnp.int32(0), []
    for k, width in enumerate(UNROLL):
        members = jnp.sum((kind == k).astype(jnp.int32))
        place = place + jnp.where(kind == k, start, 0)
        bounds += [start // width, (start + members + width - 1) // width]
        start = start + (members + 7) // 8 * 8
    place = jnp.where(kind < 4, place, -1)
    hit = place[:, None] == jnp.arange(pairs + 32, dtype=jnp.int32)[None, :]
    order = jnp.sum(jnp.where(hit, slot[:, None] + 1, 0), axis=0) - 1
    return order, jnp.stack(bounds)


def on_device(jitter, displacement, modulus, start_vec, old_home, ghost_send, pair_list, pair_count, broken):
    tiles = old_home.shape[0]
    points = jitter.shape[2]
    cap = ghost_send.shape[2]
    width_y = lax.axis_size("gy")
    anchor = old_home // tiles
    old_slot = old_home % tiles
    off_x = anchor // width_y - lax.axis_index("gx")
    off_y = anchor % width_y - lax.axis_index("gy")
    side = jnp.where(off_x == -1, 0, jnp.where(off_x == 1, 1, jnp.where(off_y == -1, 2, jnp.where(off_y == 1, 3, 4))))
    index = jnp.arange(tiles, dtype=jnp.int32)
    earlier = (side[:, None] == side[None, :]) & (index[:, None] < index[None, :])
    ranked = jnp.sum(earlier.astype(jnp.int32), axis=0)
    cell = jnp.where(side < 4, side * CAP + ranked, -1)
    hit = cell[:, None] == jnp.arange(4 * CAP, dtype=jnp.int32)[None, :]
    wanted = jnp.sum(jnp.where(hit, old_slot[:, None], 0), axis=0).reshape(4, CAP)
    requests = [jnp.pad(wanted[d : d + 1], ((0, 7), (0, 128 - CAP))) for d in range(4)]
    asked = jnp.concatenate([r[0:1] for r in exchange(requests, SIDES, 0)], axis=0)
    pick = jnp.where(side < 4, tiles + cell, old_slot)

    state = (jitter, displacement, modulus, start_vec)
    handed = pl.pallas_call(
        hand_kernel,
        out_shape=[jax.ShapeDtypeStruct((CAP, 16, points), F32)] * 4,
        in_specs=[SMEM] + [VMEM] * 4,
        out_specs=[VMEM] * 4,
        compiler_params=LIMIT,
    )(asked, *state)
    arrived = exchange(handed, SIDES, 1)
    lat = lattice(points)
    lat8 = jnp.concatenate([lat, jnp.zeros((5, points), F32)], axis=0)
    ghost_shape = jax.ShapeDtypeStruct((cap, 16, points), F32)
    local, *sends = pl.pallas_call(
        settle_kernel,
        out_shape=[jax.ShapeDtypeStruct((tiles, 16, points), F32)] + [ghost_shape] * 8,
        in_specs=[SMEM] * 2 + [VMEM] * 9,
        out_specs=[VMEM] * 9,
        scratch_shapes=[pltpu.VMEM((tiles + 4 * CAP, 16, points), F32)],
        compiler_params=LIMIT,
    )(pick, ghost_send[0], lat8, *state, *arrived)
    ghosts = exchange(sends, AROUND, 2)
    rows = tiles + 9 * cap
    scratch = [
        pltpu.VMEM((rows, 16, points), F32),
        pltpu.VMEM((rows, points, 48), F32),
        pltpu.VMEM((tiles, 3, 8, points), F32),
    ]
    image_shape = jax.ShapeDtypeStruct((tiles, 3, points), F32)
    order, bounds = by_kind(pair_list[0], pair_count[0])
    row = jnp.arange(48, dtype=jnp.int32)[:, None] % 16
    field = jnp.repeat(jnp.array(FIELDS, jnp.int32), points)[None, :]
    spread = (row == field).astype(jnp.bfloat16)
    head = (pair_list[0], order, bounds, ghost_send[0], spread, broken, local, *ghosts)
    first_image, *image_sends = pl.pallas_call(
        functools.partial(apply_kernel, True),
        out_shape=[image_shape] + [jax.ShapeDtypeStruct((cap, 8, points), F32)] * 8,
        in_specs=[SMEM] * 4 + [VMEM] * 11,
        out_specs=[VMEM] * 9,
        scratch_shapes=scratch,
        compiler_params=LIMIT,
    )(*head)
    image_ghosts = exchange(image_sends, AROUND, 3)
    second_image = pl.pallas_call(
        functools.partial(apply_kernel, False),
        out_shape=image_shape,
        in_specs=[SMEM] * 4 + [VMEM] * 20,
        out_specs=VMEM,
        scratch_shapes=scratch,
        compiler_params=LIMIT,
    )(*head, first_image, *image_ghosts)
    return (first_image, second_image)


def solution(mesh):
    split = ("gx", "gy")
    spec3, spec2, spec1 = P(split, None, None), P(split, None), P(split)
    return jax.shard_map(
        on_device,
        mesh=mesh,
        in_specs=(spec3, spec3, spec2, spec3, spec1, spec3, spec3, spec1, spec3),
        out_specs=(spec3, spec3),
        check_vma=False,
    )
```

profile of v0, /device:TPU:18, one launch (start us, length us, event | category | flops | bytes accessed | tf_op | source)
XLA Modules:
  0.0 165.4 jit_solution(2288806857812404799)
XLA Ops:
  0.6 0.0 copy-start.2
  0.6 0.0 copy-start
  0.7 0.7 compare_select_fusion.6
  1.4 0.1 convert_reduce_fusion.1
  1.5 0.7 compare_select_fusion.13
  2.2 0.1 select_reduce_fusion.1
  2.3 0.1 slice_bitcast_fusion
  2.4 4.7 %shard_map.113 = (s32[8,128]{1,0:T(8,128)S(1)}, s32[8,128]{1,0:T(8,128)S(1)}, s32[8,128]{1,0:T(8,128)S(1)}, s32[8,128]{1,0:T(8,128)S(1)}) custom-call(s32[8,128]{1,0:T(8,128)S(1)} %pad.14.refs_0_, s32[8,128]{1,0:T(8,128)S(1)} %pad.15.refs_1_, s32[8,128]{1,0:T(8,128)S(1)} %pad.16.refs_2_, s32[8,128]{1,0:T(8,128)S(1)} %pad.17.refs_3_), custom_call_target="tpu_custom_call" | custom-call | tf_op jit(solution)/shard_map/pallas_call | solution.py:275
  7.2 1.1 copy.23.jit
  8.2 0.0 copy-start.3
  8.3 1.1 copy.24.disp
  9.3 0.0 copy-done.2
  9.3 0.1 copy.25.vec
  9.5 0.0 copy-done
  9.5 0.8 shard_map.114
  10.3 8.5 %shard_map.115 = (f32[16,16,128]{2,1,0:T(8,128)S(1)}, f32[16,16,128]{2,1,0:T(8,128)S(1)}, f32[16,16,128]{2,1,0:T(8,128)S(1)}, f32[16,16,128]{2,1,0:T(8,128)S(1)}) custom-call(f32[16,16,128]{2,1,0:T(8,128)S(1)} %get-tuple-element.52.refs_0_, f32[16,16,128]{2,1,0:T(8,128)S(1)} %get-tuple-element.53.refs_1_, f32[16,16,128]{2,1,0:T(8,128)S(1)} %get-tuple-element.54.refs_2_, ...), custom_call_target="tpu_custom_call" | custom-call | tf_op jit(solution)/shard_map/pallas_call | solution.py:275
  18.9 0.0 copy-done.3
  18.9 0.0 copy-start.1
  18.9 0.0 copy-start.4
  18.9 1.6 shard_map.116
  20.6 15.5 %shard_map.117 = (f32[16,16,128]{2,1,0:T(8,128)S(1)}, f32[16,16,128]{2,1,0:T(8,128)S(1)}, f32[16,16,128]{2,1,0:T(8,128)S(1)}, f32[16,16,128]{2,1,0:T(8,128)S(1)}...) custom-call(f32[16,16,128]{2,1,0:T(8,128)S(1)} %get-tuple-element.61, ...), custom_call_target="tpu_custom_call" | custom-call | tf_op jit(solution)/shard_map/pallas_call | solution.py:275
  36.8 0.7 convert_reduce_fusion.2
  41.4 0.8 stack.38.bounds
  42.2 0.2 convert_reduce_fusion
  42.3 0.2 select_reduce_fusion
  42.6 0.1 broadcast_bitcast_fusion
  42.7 0.1 compare_convert_fusion.spread
  42.8 56.1 %shard_map.118 = (f32[128,3,128]{2,1,0:T(4,128)S(1)}, f32[16,8,128]{2,1,0:T(8,128)S(1)}, f32[16,8,128]{2,1,0:T(8,128)S(1)}, f32[16,8,128]{2,1,0:T(8,128)S(1)}, f...) custom-call(s32[4,512]{1,0:T(4,128)S(1)} %bitcast.27, ...), custom_call_target="tpu_custom_call" | custom-call | tf_op jit(solution)/shard_map/pallas_call | solution.py:364
  98.9 9.3 %shard_map.119 = (f32[16,8,128]{2,1,0:T(8,128)S(1)}, f32[16,8,128]{2,1,0:T(8,128)S(1)}, f32[16,8,128]{2,1,0:T(8,128)S(1)}, f32[16,8,128]{2,1,0:T(8,128)S(1)}, f3...) custom-call(f32[16,8,128]{2,1,0:T(8,128)S(1)} %get-tuple-element.78., ...), custom_call_target="tpu_custom_call" | custom-call | tf_op jit(solution)/shard_map/pallas_call | solution.py:275
  108.2 55.8 %shard_map.120 = f32[128,3,128]{2,1,0:T(4,128)S(1)} custom-call(s32[4,512]{1,0:T(4,128)S(1)} %bitcast.28, s32[544]{0:T(1024)S(1)} %broadcast_add_fusion.order, s32[8]{0:T(128)S(1)} %stack.38.bounds, s32[9,16]{1,0:T(8,128)S(1)} %bitcast.26, bf16[48,1280]{1,0:T(8,128)(2,1)S(1)} %compare_convert_fusion.spread, s32[512,16,128]{2,1,0:T(8,128)} %words.3, ...), custom_call_target="tpu_custom_call" | custom-call | tf_op jit(solution)/shard_map/pallas_call | solution.py:373
  164.0 0.7 copy.27
  164.7 0.7 copy.26
  (20 shorter events, 0.1 us)
Async XLA Ops:
  0.6 8.7 %copy-start.2 = (f32[128,3,128]{2,0,1:T(8,128)S(1)}, f32[128,3,128]{2,0,1:T(8,128)}, u32[]{:S(2)}) copy-start(f32[128,3,128]{2,0,1:T(8,128)} %param.13) | copy-start | bytes 589828
  0.6 8.8 %copy-start = (f32[128,128]{1,0:T(8,128)S(1)}, f32[128,128]{1,0:T(8,128)}, u32[]{:S(2)}) copy-start(f32[128,128]{1,0:T(8,128)} %mod.3) | copy-start | bytes 196612
  8.2 10.6 %copy-start.3 = (s32[1,9,16]{2,0,1:T(1,128)S(1)}, s32[1,9,16]{2,0,1:T(1,128)}, u32[]{:S(2)}) copy-start(s32[1,9,16]{2,0,1:T(1,128)} %param.15) | copy-start | bytes 1732
  18.9 17.2 %copy-start.1 = (s32[1,4,512]{2,1,0:T(4,128)S(1)}, s32[1,4,512]{2,1,0:T(4,128)}, u32[]{:S(2)}) copy-start(s32[1,4,512]{2,1,0:T(4,128)} %param.16) | copy-start | bytes 24580
  18.9 23.6 %copy-start.4 = (s32[10]{0:T(128)S(1)}, s32[10]{0:T(128)}, u32[]{:S(2)}) copy-start(s32[10]{0:T(128)} %constant.229.clone) | copy-start | bytes 124
where the time goes:
time: 166 us; the launch traced here: 165 us
  Pallas kernels  152 us (92%)
  between operations  5.44 us (3%)
  local copies, waits for them, and re-layouts  4.65 us (3%)
  other arithmetic  2.9 us (2%)
    pallas_call x1, Pallas kernels, on_device(): pl.pallas_call(functools.partial(apply_kernel, True), out_shape=[image_sh...  56.1 us
    pallas_call x1, Pallas kernels, on_device(): pl.pallas_call(functools.partial(apply_kernel, False), out_shape=image_sh...  55.8 us
    pallas_call x4, Pallas kernels, exchange(): pl.pallas_call(functools.partial(exchange_kernel, offsets), out_shape=[ja...  38 us
    unnamed x16, local copies, waits for them, and re-layouts  3.68 us

commit v1 on v0

--- a/solution.py
+++ b/solution.py
@@ -286,7 +286,7 @@
 
 SIDES = ((-1, 0), (1, 0), (0, -1), (0, 1))
 AROUND = tuple((e // 3 - 1, e % 3 - 1) for e in DIRS)
-UNROLL = (1, 4, 4, 8)
+UNROLL = (2, 8, 8, 16)
 
 
 def by_kind(pair_list, count):
@@ -301,9 +301,9 @@
         members = jnp.sum((kind == k).astype(jnp.int32))
         place = place + jnp.where(kind == k, start, 0)
         bounds += [start // width, (start + members + width - 1) // width]
-        start = start + (members + 7) // 8 * 8
+        start = start + (members + 15) // 16 * 16
     place = jnp.where(kind < 4, place, -1)
-    hit = place[:, None] == jnp.arange(pairs + 32, dtype=jnp.int32)[None, :]
+    hit = place[:, None] == jnp.arange(pairs + 64, dtype=jnp.int32)[None, :]
     order = jnp.sum(jnp.where(hit, slot[:, None] + 1, 0), axis=0) - 1
     return order, jnp.stack(bounds)
 

time: 166 us -> 151 us (0.910)
  the two profiles are of different devices: /device:TPU:18 before, /device:TPU:11 now
where the time goes in v1:
time: 151 us; the launch traced here: 149 us
  Pallas kernels  135 us (89%)
  between operations  6.27 us (4%)
  local copies, waits for them, and re-layouts  4.88 us (3%)
  other arithmetic  2.9 us (2%)
    pallas_call x1, Pallas kernels, on_device(): pl.pallas_call(functools.partial(apply_kernel, True), out_shape=[image_sh...  46.8 us
    pallas_call x1, Pallas kernels, on_device(): pl.pallas_call(functools.partial(apply_kernel, False), out_shape=image_sh...  46.4 us
    pallas_call x4, Pallas kernels, exchange(): pl.pallas_call(functools.partial(exchange_kernel, offsets), out_shape=[ja...  39.6 us
    unnamed x14, local copies, waits for them, and re-layouts  4.61 us

profile of v1, /device:TPU:11, one launch (start us, length us, event | category | flops | bytes accessed | tf_op | source)
XLA Modules:
  0.0 149.4 jit_solution(18155651543714902436)
XLA Ops:
  0.6 0.0 copy-start
  0.6 0.7 compare_select_fusion.6
  1.4 0.1 convert_reduce_fusion.1
  1.5 0.7 compare_select_fusion.13
  2.1 0.1 select_reduce_fusion.1
  2.2 0.1 slice_bitcast_fusion
  2.4 3.6 %shard_map.113 = (s32[8,128]{1,0:T(8,128)S(1)}, s32[8,128]{1,0:T(8,128)S(1)}, s32[8,128]{1,0:T(8,128)S(1)}, s32[8,128]{1,0:T(8,128)S(1)}) custom-call(s32[8,128]{1,0:T(8,128)S(1)} %pad.14.refs_0_, s32[8,128]{1,0:T(8,128)S(1)} %pad.15.refs_1_, s32[8,128]{1,0:T(8,128)S(1)} %pad.16.refs_2_, s32[8,128]{1,0:T(8,128)S(1)} %pad.17.refs_3_), custom_call_target="tpu_custom_call" | custom-call | tf_op jit(solution)/shard_map/pallas_call | solution.py:275
  6.0 1.1 copy.23.jit
  7.1 0.0 copy-start.2
  7.1 1.1 copy.24.disp
  8.2 1.1 copy.25.vec
  9.2 0.0 copy-done
  9.2 0.8 shard_map.114
  10.1 9.6 %shard_map.115 = (f32[16,16,128]{2,1,0:T(8,128)S(1)}, f32[16,16,128]{2,1,0:T(8,128)S(1)}, f32[16,16,128]{2,1,0:T(8,128)S(1)}, f32[16,16,128]{2,1,0:T(8,128)S(1)}) custom-call(f32[16,16,128]{2,1,0:T(8,128)S(1)} %get-tuple-element.52.refs_0_, f32[16,16,128]{2,1,0:T(8,128)S(1)} %get-tuple-element.53.refs_1_, f32[16,16,128]{2,1,0:T(8,128)S(1)} %get-tuple-element.54.refs_2_, ...), custom_call_target="tpu_custom_call" | custom-call | tf_op jit(solution)/shard_map/pallas_call | solution.py:275
  19.8 0.0 copy-done.2
  19.8 0.0 copy-start.1
  19.8 0.0 copy-start.3
  19.8 1.6 %shard_map.116 = (f32[128,16,128]{2,1,0:T(8,128)S(1)}, f32[16,16,128]{2,1,0:T(8,128)S(1)}, f32[16,16,128]{2,1,0:T(8,128)S(1)}, f32[16,16,128]{2,1,0:T(8,128)S(1)...) custom-call(s32[128]{0:T(128)S(1)} %get-tuple-element.102.pick, ...), custom_call_target="tpu_custom_call" | custom-call | tf_op jit(solution)/shard_map/pallas_call | solution.py:343
  21.5 18.2 %shard_map.117 = (f32[16,16,128]{2,1,0:T(8,128)S(1)}, f32[16,16,128]{2,1,0:T(8,128)S(1)}, f32[16,16,128]{2,1,0:T(8,128)S(1)}, f32[16,16,128]{2,1,0:T(8,128)S(1)}...) custom-call(f32[16,16,128]{2,1,0:T(8,128)S(1)} %get-tuple-element.61, ...), custom_call_target="tpu_custom_call" | custom-call | tf_op jit(solution)/shard_map/pallas_call | solution.py:275
  39.7 0.0 copy-done.1
  40.3 0.7 convert_reduce_fusion.2
  45.8 0.1 stack.38.bounds
  45.9 0.2 convert_reduce_fusion
  46.1 0.2 select_reduce_fusion
  46.3 0.0 copy-done.3
  46.3 0.1 broadcast_bitcast_fusion
  46.4 0.1 compare_convert_fusion.spread
  46.5 46.8 %shard_map.118 = (f32[128,3,128]{2,1,0:T(4,128)S(1)}, f32[16,8,128]{2,1,0:T(8,128)S(1)}, f32[16,8,128]{2,1,0:T(8,128)S(1)}, f32[16,8,128]{2,1,0:T(8,128)S(1)}, f...) custom-call(s32[4,512]{1,0:T(4,128)S(1)} %bitcast.27, ...), custom_call_target="tpu_custom_call" | custom-call | tf_op jit(solution)/shard_map/pallas_call | solution.py:364
  93.3 8.3 %shard_map.119 = (f32[16,8,128]{2,1,0:T(8,128)S(1)}, f32[16,8,128]{2,1,0:T(8,128)S(1)}, f32[16,8,128]{2,1,0:T(8,128)S(1)}, f32[16,8,128]{2,1,0:T(8,128)S(1)}, f3...) custom-call(f32[16,8,128]{2,1,0:T(8,128)S(1)} %get-tuple-element.78., ...), custom_call_target="tpu_custom_call" | custom-call | tf_op jit(solution)/shard_map/pallas_call | solution.py:275
  101.6 46.4 %shard_map.120 = f32[128,3,128]{2,1,0:T(4,128)S(1)} custom-call(s32[4,512]{1,0:T(4,128)S(1)} %bitcast.28, s32[576]{0:T(1024)S(1)} %broadcast_add_fusion.order, s32[8]{0:T(128)S(1)} %stack.38.bounds, s32[9,16]{1,0:T(8,128)S(1)} %bitcast.26, bf16[48,1280]{1,0:T(8,128)(2,1)S(1)} %compare_convert_fusion.spread, s32[512,16,128]{2,1,0:T(8,128)} %words.3, ...), custom_call_target="tpu_custom_call" | custom-call | tf_op jit(solution)/shard_map/pallas_call | solution.py:373
  148.0 0.7 copy.27
  148.7 0.7 copy.26
  (18 shorter events, 0.1 us)
Async XLA Ops:
  0.6 8.6 %copy-start = (f32[128,128]{1,0:T(8,128)S(1)}, f32[128,128]{1,0:T(8,128)}, u32[]{:S(2)}) copy-start(f32[128,128]{1,0:T(8,128)} %mod.3) | copy-start | bytes 196612
  7.1 12.7 %copy-start.2 = (s32[1,9,16]{2,0,1:T(1,128)S(1)}, s32[1,9,16]{2,0,1:T(1,128)}, u32[]{:S(2)}) copy-start(s32[1,9,16]{2,0,1:T(1,128)} %param.15) | copy-start | bytes 1732
  19.8 19.9 %copy-start.1 = (s32[1,4,512]{2,1,0:T(4,128)S(1)}, s32[1,4,512]{2,1,0:T(4,128)}, u32[]{:S(2)}) copy-start(s32[1,4,512]{2,1,0:T(4,128)} %param.16) | copy-start | bytes 24580
  19.8 26.5 %copy-start.3 = (s32[10]{0:T(128)S(1)}, s32[10]{0:T(128)}, u32[]{:S(2)}) copy-start(s32[10]{0:T(128)} %constant.229.clone) | copy-start | bytes 124
